TPU v7x, 512 devices: a whole 4x4x16 slice. The times are simulated.
512 devices in a mesh: replica: 32 (over z, y_hi), tensor: 16 (over y_lo, x, core).
Axes of the slice: x: 4, y: 4 (y_hi: 2, y_lo: 2; y = y_hi * 2 + y_lo), z: 16, core: 2. Of those that a mesh axis runs over, the one named last changes fastest.
Arguments:
- key_head_weight: bfloat16 [16, 128, 8192], P('tensor'), may hold values from -6 to 6
- down_factor_slots: float32 [32, 2, 8192], P('replica', None, 'tensor'), may hold values from -6 to 6
- adapter_up_factor: float32 [64, 1024], P('replica'), may hold values from -0.2 to 0.2
- piece_slot_index: int32 [32], replicated, may hold values from 0 to 31, each once
Outputs:
- merged: bfloat16 [16, 128, 8192], P('tensor')
Inputs may be any that keep to these rules, and one draw needn't show every extreme that they name: Piece p lies in slot piece_slot_index[p] of down_factor_slots; every slot holds exactly one piece.
All inputs are finite; a program needn't handle non-finite values.
Results may differ from a plain program's by a relative error of at most 0.001.
Values sent between devices are 32-bit elements; how exact they have to be, the bound alone decides.
A program may use at most 64 MiB of HBM per device.

v0:
```python
import jax
import jax.numpy as jnp
from jax import lax
from jax.sharding import PartitionSpec as P

KV_HEADS = 8
merge_scale = 2.0


def arrange_pieces(slot_row_count, piece_slot_index, factor_rank):
    ordered = jnp.take(slot_row_count, piece_slot_index, axis=0)
    return ordered.reshape(factor_rank, ordered.shape[-1])


def merge_weight_block(resident_block, down_factor_rows, adapter_rows):
    lowrank_update = jnp.dot(
        adapter_rows.T,
        down_factor_rows,
        preferred_element_type=jnp.float32,
        precision=lax.Precision.HIGHEST,
    )
    return (resident_block.astype(jnp.float32) + merge_scale * lowrank_update[None]).astype(
        jnp.bfloat16
    )


def local(key_head_weight, down_factor_slots, adapter_up_factor, piece_slot_index):
    output_units = key_head_weight.shape[1]
    copies = max(1, lax.axis_size("tensor") // KV_HEADS)
    first_index = lax.axis_index("tensor") // copies * output_units
    adapter_columns = lax.dynamic_slice_in_dim(adapter_up_factor, first_index, output_units, 1)
    owner_rows = lax.all_gather(down_factor_slots, "tensor", axis=2, tiled=True)
    slot_row_count, adapter_rows = (
        lax.all_gather(owner_rows, "replica", axis=0, tiled=True),
        lax.all_gather(adapter_columns, "replica", axis=0, tiled=True),
    )
    down_factor_rows = arrange_pieces(slot_row_count, piece_slot_index, adapter_rows.shape[0])
    return merge_weight_block(key_head_weight, down_factor_rows, adapter_rows)


def solution(mesh):
    in_specs = (P("tensor", None, None), P("replica", None, "tensor"), P("replica", None), P())
    out_specs = P("tensor", None, None)
    return jax.shard_map(local, mesh=mesh, in_specs=in_specs, out_specs=out_specs, check_vma=False)
```

profile of v0, /device:TPU:2, one launch (start us, length us, event | category | flops | bytes accessed | tf_op | source)
XLA Modules:
  0.0 201.6 jit_solution(13053699690656250366)
XLA Ops:
  6.5 0.0 copy-start
  6.5 0.0 all-gather.3.cloned.1.call-start
  6.5 23.7 %all_gather.10 = f32[1,2,8192]{2,1,0:T(2,128)} all-gather(f32[1,2,512]{2,1,0:T(2,128)} %param.5), channel_id=1, replica_groups=mesh['replica'=32,'tensor'=16] {'tensor'}, dimensions={2}, use_global_device_ids=true | all-gather | bytes 69632 | tf_op jit(solution)/shard_map/all_gather | solution.py:32
  30.3 0.0 all-gather.3.cloned.1.call-update
  30.3 0.7 compare_and_fusion
  31.0 0.1 broadcast_in_dim.17
  31.0 0.1 broadcast_in_dim.18
  31.2 0.0 copy-done
  31.2 77.4 %all-gather = f32[32,2,128]{2,1,0:T(2,128)S(1)} all-gather(f32[1,2,128]{2,1,0:T(2,128)S(1)} %dynamic-slice_bitcast_fusion), channel_id=1, replica_groups=mesh['replica'=32,'tensor'=16] {'replica'}, dimensions={0}, use_global_device_ids=true | all-gather | bytes 33792 | tf_op jit(solution)/shard_map/all_gather | solution.py:35
  108.6 0.7 compare_select_fusion
  109.2 70.9 %all-gather.3.cloned.1.call-done = f32[32,2,8192]{2,1,0:T(2,128)} async-done(((f32[1,2,8192]{2,1,0:T(2,128)}), f32[32,2,8192]{2,1,0:T(2,128)}) %all-gather.3.cloned.1.call-update) | async-done | bytes 2097168 | tf_op jit(solution)/shard_map/all_gather | solution.py:34
  180.2 5.6 %gather_fusion = f32[32,2,8192]{2,1,0:T(2,128)} fusion(f32[32,2,8192]{2,1,0:T(2,128)} %all-gather.3.cloned.1.call-done, s32[1024]{0:T(1024)S(1)} %pad_clamp_fusion), kind=kCustom, calls=%fused_computation | custom fusion | bytes 4194432 | tf_op jit(solution)/shard_map/jit(_take)/gather | solution.py:11
  185.7 2.7 %gather.7 = f32[64,8192]{1,0:T(8,128)S(1)} reshape(f32[32,2,8192]{2,1,0:T(2,128)} %gather_fusion) | data formatting | bytes 4194304 | tf_op jit(solution)/shard_map/jit(_take)/gather | solution.py:11
  188.4 6.4 %fusion.2 = bf16[1,128,8192]{2,1,0:T(8,128)(2,1)} fusion(f32[64,128]{1,0:T(8,128)S(1)} %bitcast.10, bf16[1,128,8192]{2,1,0:T(8,128)(2,1)} %param.4, f32[64,8192]{1,0:T(8,128)S(1)} %gather.7, pred[64]{0:T(512)(128)(4,1)S(1)} %broadcast_in_dim.18), kind=kOutput, calls=%fused_computation.4 | convolution fusion | flops 810024960 | bytes 6324288 | tf_op jit(solution)/shard_map/dot_general | solution.py:16
  (2 shorter events, 0.0 us)
Async XLA Ops:
  6.5 24.6 %copy-start = (f32[2,1024]{1,0:T(2,128)S(1)}, f32[2,1024]{1,0:T(2,128)}, u32[]{:S(2)}) copy-start(f32[2,1024]{1,0:T(2,128)} %param.6) | copy-start | bytes 24580
  6.5 173.6 %all-gather.3.cloned.1.call-start = ((), (), s32[]{:S(2)}) async-start(), calls=%async_computation | async-start | bytes 2162688 | tf_op jit(solution)/shard_map/all_gather | solution.py:34
Sparse Core Ops, SparseCore 0:
  30.4 149.7 all-gather.2
where the time goes:
time: 202 us
  blocking collectives  101 us (50%)
  waiting for transfers between devices  70.9 us (35%)
  between operations  13.4 us (7%)
  local copies, waits for them, and re-layouts  8.46 us (4%)
  matrix products  6.37 us (3%)
    all_gather x1, blocking collectives, local(): lax.all_gather(adapter_columns, 'replica', axis=0, tiled=True)  77.4 us
    all_gather x1, waiting for transfers between devices, local(): lax.all_gather(owner_rows, 'replica', axis=0, tiled=True)  70.9 us
    all_gather x1, blocking collectives, local(): owner_rows = lax.all_gather(down_factor_slots, 'tensor', axis=2, tiled=True)  23.7 us
    gather x2, local copies, waits for them, and re-layouts, arrange_pieces(): ordered = jnp.take(slot_row_count, piece_slot_index, axis=0)  8.26 us
    dot_general x1, matrix products, merge_weight_block(): jnp.dot(adapter_rows.T, down_factor_rows, preferred_element_type=jnp.floa...  6.37 us
  transfers between devices with their start and end apart: 1, of which 1 were waited for; matrix products, arithmetic and copies ran while one was open for 1% of the time, Pallas kernels for 0%

commit v1 on v0

--- a/solution.py
+++ b/solution.py
@@ -29,7 +29,10 @@
     copies = max(1, lax.axis_size("tensor") // KV_HEADS)
     first_index = lax.axis_index("tensor") // copies * output_units
     adapter_columns = lax.dynamic_slice_in_dim(adapter_up_factor, first_index, output_units, 1)
-    owner_rows = lax.all_gather(down_factor_slots, "tensor", axis=2, tiled=True)
+    owner_rows = jnp.concatenate(
+        lax.all_to_all(jnp.stack([down_factor_slots] * lax.axis_size("tensor")), "tensor", 0, 0),
+        axis=2,
+    )
     slot_row_count, adapter_rows = (
         lax.all_gather(owner_rows, "replica", axis=0, tiled=True),
         lax.all_gather(adapter_columns, "replica", axis=0, tiled=True),

time: 202 us -> 193 us (0.955)
  blocking collectives: 101 us -> 92.8 us
    all_gather x1 -> x0, blocking collectives: 23.7 us -> none  [local(): owner_rows = lax.all_gather(down_factor_slots, 'tensor', axis=2, tiled=True)]
    all_to_all x0 -> x1, blocking collectives: none -> 13.8 us  [local(): lax.all_to_all(jnp.stack([down_factor_slots] * lax.axis_size('tensor')),...]
where the time goes in v1:
time: 193 us
  blocking collectives  92.8 us (48%)
  waiting for transfers between devices  69.8 us (36%)
  between operations  13.4 us (7%)
  local copies, waits for them, and re-layouts  9.17 us (5%)
  matrix products  6.37 us (3%)
    all_gather x1, blocking collectives, local(): lax.all_gather(adapter_columns, 'replica', axis=0, tiled=True)  79 us
    all_gather x1, waiting for transfers between devices, local(): lax.all_gather(owner_rows, 'replica', axis=0, tiled=True)  69.8 us
    all_to_all x1, blocking collectives, local(): lax.all_to_all(jnp.stack([down_factor_slots] * lax.axis_size('tensor')),...  13.8 us
    gather x2, local copies, waits for them, and re-layouts, arrange_pieces(): ordered = jnp.take(slot_row_count, piece_slot_index, axis=0)  8.26 us
    dot_general x1, matrix products, merge_weight_block(): jnp.dot(adapter_rows.T, down_factor_rows, preferred_element_type=jnp.floa...  6.37 us
  transfers between devices with their start and end apart: 1, of which 1 were waited for; matrix products, arithmetic and copies ran while one was open for 1% of the time, Pallas kernels for 0%

profile of v1, /device:TPU:2, one launch (start us, length us, event | category | flops | bytes accessed | tf_op | source)
XLA Modules:
  0.0 192.9 jit_solution(11286800726962515689)
XLA Ops:
  6.5 0.0 copy-start
  6.5 0.0 all-gather.3.cloned.1.call-start
  6.5 0.7 stack.2
  7.3 13.8 %all_to_all.5 = f32[16,1,2,512]{3,2,1,0:T(2,128)} all-to-all(f32[16,1,2,512]{3,2,1,0:T(2,128)S(1)} %stack.2), channel_id=1, replica_groups=mesh['replica'=32,'tensor'=16] {'tensor'}, dimensions={0} | all-to-all | bytes 131072 | tf_op jit(solution)/shard_map/all_to_all | solution.py:33
  21.1 0.0 all-gather.3.cloned.1.call-update
  21.1 0.7 compare_and_fusion
  21.8 0.1 broadcast_in_dim.17
  21.9 0.1 broadcast_in_dim.18
  22.0 0.0 copy-done
  22.0 79.0 %all-gather = f32[32,2,128]{2,1,0:T(2,128)S(1)} all-gather(f32[1,2,128]{2,1,0:T(2,128)S(1)} %dynamic-slice_bitcast_fusion), channel_id=1, replica_groups=mesh['replica'=32,'tensor'=16] {'replica'}, dimensions={0}, use_global_device_ids=true | all-gather | bytes 33792 | tf_op jit(solution)/shard_map/all_gather | solution.py:38
  101.0 0.7 compare_select_fusion
  101.7 69.8 %all-gather.3.cloned.1.call-done = f32[32,2,8192]{2,1,0:T(2,128)} async-done(((f32[1,2,8192]{2,1,0:T(2,128)}), f32[32,2,8192]{2,1,0:T(2,128)}) %all-gather.3.cloned.1.call-update) | async-done | bytes 2097168 | tf_op jit(solution)/shard_map/all_gather | solution.py:37
  171.4 5.6 %gather_fusion = f32[32,2,8192]{2,1,0:T(2,128)} fusion(f32[32,2,8192]{2,1,0:T(2,128)} %all-gather.3.cloned.1.call-done, s32[1024]{0:T(1024)S(1)} %pad_clamp_fusion), kind=kCustom, calls=%fused_computation | custom fusion | bytes 4194432 | tf_op jit(solution)/shard_map/jit(_take)/gather | solution.py:11
  177.0 2.7 %gather.7 = f32[64,8192]{1,0:T(8,128)S(1)} reshape(f32[32,2,8192]{2,1,0:T(2,128)} %gather_fusion) | data formatting | bytes 4194304 | tf_op jit(solution)/shard_map/jit(_take)/gather | solution.py:11
  179.7 6.4 %fusion.2 = bf16[1,128,8192]{2,1,0:T(8,128)(2,1)} fusion(f32[64,128]{1,0:T(8,128)S(1)} %bitcast.15, bf16[1,128,8192]{2,1,0:T(8,128)(2,1)} %param.4, f32[64,8192]{1,0:T(8,128)S(1)} %gather.7, pred[64]{0:T(512)(128)(4,1)S(1)} %broadcast_in_dim.18), kind=kOutput, calls=%fused_computation.4 | convolution fusion | flops 810024960 | bytes 6324288 | tf_op jit(solution)/shard_map/dot_general | solution.py:16
  (2 shorter events, 0.0 us)
Async XLA Ops:
  6.5 15.5 %copy-start = (f32[2,1024]{1,0:T(2,128)S(1)}, f32[2,1024]{1,0:T(2,128)}, u32[]{:S(2)}) copy-start(f32[2,1024]{1,0:T(2,128)} %param.6) | copy-start | bytes 24580
  6.5 164.9 %all-gather.3.cloned.1.call-start = ((), (), s32[]{:S(2)}) async-start(), calls=%async_computation.1 | async-start | bytes 2162688 | tf_op jit(solution)/shard_map/all_gather | solution.py:37
Sparse Core Ops, SparseCore 0:
  21.2 150.1 all-gather.2
